TPU v7x, 128 devices: a whole 4x4x4 slice. The times are simulated.
128 devices in a mesh: dp: 4 (over x), outer: 16 (over z, y), inner: 2 (over core).
Axes of the slice: x: 4, y: 4, z: 4, core: 2. Of those that a mesh axis runs over, the one named last changes fastest.
Arguments:
- queries: bfloat16 [4, 4096, 1024], P('dp', ('outer', 'inner')), may hold values from -6 to 6
- keys: bfloat16 [4, 4096, 2, 1024], P('dp', ('outer', 'inner')), may hold values from -6 to 6
- values: bfloat16 [4, 4096, 2, 1024], P('dp', ('outer', 'inner')), may hold values from -6 to 6
- betas: float32 [4, 8, 2, 4096], P('dp', None, None, ('outer', 'inner')), may hold values from 0.3 to 1.6
- grad_out: bfloat16 [4, 4096, 1024], P('dp', ('outer', 'inner')), may hold values from -16 to 16
- gain: float32 [1024], replicated, may hold values from 0.1 to 1.9
Outputs:
- grad_queries: bfloat16 [4, 4096, 1024], P('dp', ('outer', 'inner'))
- grad_keys: bfloat16 [4, 4096, 2, 1024], P('dp', ('outer', 'inner'))
- grad_values: bfloat16 [4, 4096, 2, 1024], P('dp', ('outer', 'inner'))
- gain_grad: float32 [1024], replicated
All inputs are finite; a program needn't handle non-finite values.
Results may differ from a plain program's by a relative error of at most 0.001.
Values sent between devices are 32-bit elements; how exact they have to be, the bound alone decides.
A program may use at most 128 MiB of HBM per device.

v0:
```python
import math
import jax
import jax.numpy as jnp
from jax import lax
from jax.sharding import PartitionSpec as P

HEADS = 8
HEAD_DIM = 128
STRETCH = 64
EXACT = lax.Precision.HIGHEST
EPS_KEY = 1e-06
EPS_OUT = 1e-05


def passed_along(block, axis, distance):
    devices = range(lax.axis_size(axis))
    route = [(i - distance, i) for i in devices if i - distance in devices]
    return lax.ppermute(block, axis, route)


def spread(value, axis, source):
    kept = jnp.where(lax.axis_index(axis) == source, value, 0).astype(value.dtype)
    return lax.psum(kept, axis)


def prefix(shard, axis, combine, identity, reverse):
    size, here = (lax.axis_size(axis), lax.axis_index(axis))
    everything = lax.all_gather(shard, axis)
    start = jnp.broadcast_to(jnp.asarray(identity, shard.dtype), shard.shape)

    def step(k, before):
        at = size - 1 - k if reverse else k
        reached = at > here if reverse else at < here
        new = combine(before, everything[at])
        return jnp.where(reached, new, before)

    return lax.fori_loop(0, size, step, start)


def product(spec, left, right):
    return jnp.einsum(spec, left, right, precision=EXACT, preferred_element_type=jnp.float32)


def unit_rows(raw):
    scale_inv = lax.rsqrt(jnp.sum(raw * raw, axis=-1, keepdims=True) + EPS_KEY)
    return (raw * scale_inv, scale_inv)


def unit_back(unit, scale_inv, grad):
    return scale_inv * (grad - unit * jnp.sum(unit * grad, axis=-1, keepdims=True))


def compose(earlier, later):
    through = product("mhij,hjk->mhik", earlier, later[0])
    return through + jnp.stack([jnp.zeros_like(later[1]), later[1]])


def stretch_factors(key_blk, value_blk, rate_blk, strict, eye_refl, eye_head):
    head_dim = key_blk.shape[2]
    gram = product("hrd,hsd->hrs", key_blk, key_blk)
    lower_mat = eye_refl + rate_blk[:, :, None] * gram * strict
    rhs = jnp.concatenate(
        [rate_blk[:, :, None] * key_blk, rate_blk[:, :, None] * value_blk], axis=2
    )
    solved = jax.scipy.linalg.solve_triangular(lower_mat, rhs, lower=True)
    w_mat = solved[:, :, :head_dim]
    t_vals = solved[:, :, head_dim:]
    transit = eye_head - product("hrd,hre->hde", w_mat, key_blk)
    return (lower_mat, w_mat, t_vals, transit)


def forward_nested(own_map, identity):
    count = lax.axis_size("inner")
    first = lax.axis_index("inner") == 0
    acc_map = identity
    sent = compose(acc_map, own_map)
    got = passed_along(sent, "inner", 1)
    acc_map = jnp.stack([jnp.where(first, identity[0], got[0]), got[1]])
    group_map = spread(compose(acc_map, own_map), "inner", count - 1)
    before = prefix(group_map, "outer", compose, identity, False)
    return compose(before, acc_map)


def backward_nested(own_map, identity):
    count = lax.axis_size("inner")
    final = lax.axis_index("inner") == count - 1
    acc_map = identity
    sent = compose(acc_map, own_map)
    got = passed_along(sent, "inner", -1)
    acc_map = jnp.stack([jnp.where(final, identity[0], got[0]), got[1]])
    group_map = spread(compose(acc_map, own_map), "inner", 0)
    after = prefix(group_map, "outer", compose, identity, True)
    return compose(after, acc_map)


def on_device(queries, keys, values, betas, grad_out, gain):
    length_here = queries.shape[1]
    heads = HEADS
    head_dim = HEAD_DIM
    span = STRETCH
    refl = 2 * span
    count = length_here // span
    query_raw = (
        queries[0].astype(jnp.float32).reshape(length_here, heads, head_dim).transpose(1, 0, 2)
    )
    key_raw = (
        keys[0]
        .astype(jnp.float32)
        .reshape(length_here, 2, heads, head_dim)
        .transpose(2, 0, 1, 3)
        .reshape(heads, 2 * length_here, head_dim)
    )
    value_all = (
        values[0]
        .astype(jnp.float32)
        .reshape(length_here, 2, heads, head_dim)
        .transpose(2, 0, 1, 3)
        .reshape(heads, 2 * length_here, head_dim)
    )
    rate_all = betas[0].transpose(0, 2, 1).reshape(heads, 2 * length_here)
    cotan_all = (
        grad_out[0].astype(jnp.float32).reshape(length_here, heads, head_dim).transpose(1, 0, 2)
    )
    gains = gain.reshape(heads, head_dim)
    query_n, query_inv = unit_rows(query_raw)
    key_n, key_inv = unit_rows(key_raw)
    token_ids = lax.broadcasted_iota(jnp.int32, (span, refl), 0)
    refl_ids = lax.broadcasted_iota(jnp.int32, (span, refl), 1)
    read_mask = (refl_ids <= 2 * token_ids + 1).astype(jnp.float32)
    row_ids = lax.broadcasted_iota(jnp.int32, (refl, refl), 0)
    col_ids = lax.broadcasted_iota(jnp.int32, (refl, refl), 1)
    strict = (col_ids < row_ids).astype(jnp.float32)
    eye_refl = jnp.eye(refl, dtype=jnp.float32)
    eye_head = jnp.eye(head_dim, dtype=jnp.float32)
    identity = jnp.stack(
        [
            jnp.broadcast_to(eye_head, (heads, head_dim, head_dim)),
            jnp.zeros((heads, head_dim, head_dim), jnp.float32),
        ]
    )

    def refl_rows(array, block_id):
        return array[:, block_id * refl : (block_id + 1) * refl]

    def token_rows(array, block_id):
        return array[:, block_id * span : (block_id + 1) * span]

    stash = []
    block_map = identity
    for block_id in range(count):
        key_blk = refl_rows(key_n, block_id)
        factor_set = stretch_factors(
            key_blk,
            refl_rows(value_all, block_id),
            refl_rows(rate_all, block_id),
            strict,
            eye_refl,
            eye_head,
        )
        offset = product("hrv,hre->hve", factor_set[2], key_blk)
        block_map = compose(block_map, jnp.stack([factor_set[3], offset]))
        stash.append(factor_set)

    def factors_of(block_id):
        return stash[block_id]

    state = forward_nested(block_map, identity)[1]
    records = []
    adjoint_maps = []
    gain_sum = jnp.zeros((heads, head_dim), jnp.float32)
    for block_id in range(count):
        lower_mat, w_mat, t_vals, transit = factors_of(block_id)
        key_blk = refl_rows(key_n, block_id)
        query_blk = token_rows(query_n, block_id)
        cotan_blk = token_rows(cotan_all, block_id)
        update = t_vals - product("hrk,hvk->hrv", w_mat, state)
        scores = product("htd,hrd->htr", query_blk, key_blk) * read_mask
        output = product("htk,hvk->htv", query_blk, state) + product("htr,hrv->htv", scores, update)
        scale_inv = lax.rsqrt(jnp.mean(output * output, axis=2, keepdims=True) + EPS_OUT)
        normed = output * scale_inv
        scaled = cotan_blk * gains[:, None, :]
        d_out = scale_inv * (scaled - normed * jnp.mean(normed * scaled, axis=2, keepdims=True))
        gain_sum = gain_sum + jnp.sum(cotan_blk * normed, axis=1)
        source = product("htv,htk->hvk", d_out, query_blk - product("htr,hrk->htk", scores, w_mat))
        records.append((state, update, scores, d_out))
        adjoint_maps.append(jnp.stack([jnp.swapaxes(transit, 1, 2), source]))
        state = state + product("hrv,hrk->hvk", update, key_blk)
    adjoint_block = identity
    for block_id in reversed(range(count)):
        adjoint_block = compose(adjoint_block, adjoint_maps[block_id])
    adjoint = backward_nested(adjoint_block, identity)[1]
    grad_q_parts = [None] * count
    grad_k_parts = [None] * count
    grad_v_parts = [None] * count
    for block_id in reversed(range(count)):
        lower_mat, w_mat, t_vals, transit = factors_of(block_id)
        start_state, update, scores, d_out = records[block_id]
        key_blk = refl_rows(key_n, block_id)
        query_blk = token_rows(query_n, block_id)
        rate_blk = refl_rows(rate_all, block_id)
        d_update = product("htr,htv->hrv", scores, d_out) + product(
            "hrk,hvk->hrv", key_blk, adjoint
        )
        solved = jax.scipy.linalg.solve_triangular(lower_mat, d_update, trans=1, lower=True)
        d_target = rate_blk[:, :, None] * solved
        d_scores = product("htv,hrv->htr", d_out, update) * read_mask
        grad_q_parts[block_id] = product("htv,hvk->htk", d_out, start_state) + product(
            "htr,hrk->htk", d_scores, key_blk
        )
        d_gram = -product("hrv,hsv->hrs", d_target, update) * strict
        grad_k_parts[block_id] = (
            product("hrv,hvk->hrk", update, adjoint)
            + product("htr,htk->hrk", d_scores, query_blk)
            - product("hrv,hvk->hrk", d_target, start_state)
            + product("hrs,hsk->hrk", d_gram + jnp.swapaxes(d_gram, 1, 2), key_blk)
        )
        grad_v_parts[block_id] = d_target
        adjoint = (
            adjoint
            + product("htv,htk->hvk", d_out, query_blk)
            - product("hrv,hrk->hvk", d_target, key_blk)
        )
    grad_qn = jnp.concatenate(grad_q_parts, axis=1)
    grad_kn = jnp.concatenate(grad_k_parts, axis=1)
    grad_val = jnp.concatenate(grad_v_parts, axis=1)
    grad_q = unit_back(query_n, query_inv, grad_qn)
    grad_k = unit_back(key_n, key_inv, grad_kn)
    grad_q = (
        grad_q.transpose(1, 0, 2).reshape(1, length_here, heads * head_dim).astype(jnp.bfloat16)
    )
    grad_k = (
        grad_k.reshape(heads, length_here, 2, head_dim)
        .transpose(1, 2, 0, 3)
        .reshape(1, length_here, 2, heads * head_dim)
        .astype(jnp.bfloat16)
    )
    grad_val = (
        grad_val.reshape(heads, length_here, 2, head_dim)
        .transpose(1, 2, 0, 3)
        .reshape(1, length_here, 2, heads * head_dim)
        .astype(jnp.bfloat16)
    )
    total = lax.psum(gain_sum, ("dp", "outer", "inner"))
    tokens_all = length_here * lax.axis_size("dp") * lax.axis_size("outer") * lax.axis_size("inner")
    gain_grad = total.reshape(heads * head_dim) * (1.0 / math.sqrt(tokens_all))
    return (grad_q, grad_k, grad_val, gain_grad)


def solution(mesh):
    return jax.shard_map(
        on_device,
        mesh=mesh,
        in_specs=(
            P("dp", ("outer", "inner"), None),
            P("dp", ("outer", "inner"), None, None),
            P("dp", ("outer", "inner"), None, None),
            P("dp", None, None, ("outer", "inner")),
            P("dp", ("outer", "inner"), None),
            P(),
        ),
        out_specs=(
            P("dp", ("outer", "inner"), None),
            P("dp", ("outer", "inner"), None, None),
            P("dp", ("outer", "inner"), None, None),
            P(),
        ),
        check_vma=False,
    )
```

profile of v0, /device:TPU:1, one launch (start us, length us, event | category | flops | bytes accessed | tf_op | source)
XLA Modules:
  0.0 764.0 jit_solution(11340195129437190525)
XLA Ops:
  13.8 79.8 %custom-call.9 = f32[8,1,128,128]{2,3,1,0:T(8,128)} custom-call(f32[8,1,128,128]{3,2,1,0:T(8,128)S(1)} %fusion.54), custom_call_target="InvertDiagBlocksLowerTriangular" | custom-call | tf_op jit(solution)/shard_map/jit(_solve_triangular)/vmap()/triangular_solve | solution.py:65
  103.9 79.4 %custom-call.8 = f32[8,1,128,128]{2,3,1,0:T(8,128)} custom-call(f32[8,1,128,128]{3,2,1,0:T(8,128)S(1)} %fusion.59), custom_call_target="InvertDiagBlocksLowerTriangular" | custom-call | tf_op jit(solution)/shard_map/jit(_solve_triangular)/vmap()/triangular_solve | solution.py:65
  196.4 3.9 collective-permute-done
  201.6 3.4 fusion.47
  205.1 28.1 %all-reduce.14.cloned.1.call-done = f32[1,2,8,128,128]{4,3,2,1,0:T(8,128)} async-done(((f32[1,2,8,128,128]{4,3,2,1,0:T(8,128)}), f32[1,2,8,128,128]{4,3,2,1,0:T(8,128)}) %all-reduce.14.cloned.1.call-update) | async-done | bytes 1048592 | tf_op jit(solution)/shard_map/psum | solution.py:23
  247.2 100.7 %all-gather.3.cloned.1.call-done = f32[16,2,8,128,128]{4,3,2,1,0:T(8,128)} async-done(((f32[1,2,8,128,128]{4,3,2,1,0:T(8,128)}), f32[16,2,8,128,128]{4,3,2,1,0:T(8,128)}) %all-gather.3.cloned.1.call-update) | async-done | bytes 16777232 | tf_op jit(solution)/shard_map/all_gather | solution.py:28
  347.9 89.7 %while.28 = (s32[]{:T(128)}, f32[2,8,128,128]{2,3,1,0:T(8,128)}, s32[]{:T(128)}, f32[16,2,8,128,128]{4,3,2,1,0:T(8,128)}, s32[]{:T(128)}, /*index=5*/s32[]{:T(128)}, s32[]{}) while((s32[]{:T(128)}, f32[2,8,128,128]{2,3,1,0:T(8,128)}, s32[]{:T(128)}, f32[16,2,8,128,128]{4,3,2,1,0:T(8,128)}, s32[]{:T(128)}, /*index=5*/s32[]{:T(128)}, s32[]{}) %tuple.94), condition=%wide.region_4.6_spmd, body=%wide.region_3.5_spmd.sunk | while | flops 403177472 | bytes 8389227 | solution.py:37
  350.4 3.1 fusion.235
  356.0 3.1 fusion.235
  361.6 3.1 fusion.235
  367.2 3.1 fusion.235
  372.8 3.1 fusion.235
  378.4 3.1 fusion.235
  383.9 3.1 fusion.235
  389.5 3.1 fusion.235
  395.1 3.1 fusion.235
  400.7 3.1 fusion.235
  406.3 3.1 fusion.235
  411.9 3.1 fusion.235
  417.4 3.1 fusion.235
  423.0 3.1 fusion.235
  428.6 3.1 fusion.235
  434.2 3.1 fusion.235
  437.7 3.5 convolution_bitcast_fusion.5
  473.9 25.0 %all-reduce.16.cloned.1.call-done = f32[1,2,8,128,128]{4,3,2,1,0:T(8,128)} async-done(((f32[1,2,8,128,128]{4,3,2,1,0:T(8,128)}), f32[1,2,8,128,128]{4,3,2,1,0:T(8,128)}) %all-reduce.16.cloned.1.call-update) | async-done | bytes 1048592 | tf_op jit(solution)/shard_map/psum | solution.py:23
  509.4 6.4 fusion.65
  517.5 68.1 %psum.23 = f32[8,128]{1,0:T(8,128)S(1)} all-reduce(f32[8,128]{1,0:T(8,128)S(1)} %add.275), channel_id=1, replica_groups=mesh['dp'=4,'outer'=16,'inner'=2] {'dp','outer','inner'}, use_global_device_ids=true, to_apply=%region_16.19 | all-reduce | flops 1024 | bytes 8192 | tf_op jit(solution)/shard_map/psum | solution.py:243
  597.6 17.5 %all-gather.5.cloned.1.call-done = f32[16,2,8,128,128]{4,3,2,1,0:T(8,128)} async-done(((f32[1,2,8,128,128]{4,3,2,1,0:T(8,128)}), f32[16,2,8,128,128]{4,3,2,1,0:T(8,128)}) %all-gather.5.cloned.1.call-update) | async-done | bytes 16777232 | tf_op jit(solution)/shard_map/all_gather | solution.py:28
  615.1 56.1 %while.29 = (s32[]{:T(128)}, f32[2,8,128,128]{2,3,1,0:T(8,128)S(1)}, s32[]{:T(128)}, f32[16,2,8,128,128]{4,3,2,1,0:T(8,128)}, s32[]{:T(128)}, /*index=5*/s32[]{:T(128)}, s32[]{:T(128)}, s32[]{:T(128)}, s32[]{}) while((s32[]{:T(128)}, f32[2,8,128,128]{2,3,1,0:T(8,128)S(1)}, s32[]{:T(128)}, f32[16,2,8,128,128]{4,3,2,1,0:T(8,128)}, ...), condition=%wide.region_12.14_spmd, body=%wide.region_11.13_spmd.sunk | while | flops 403177472 | bytes 8388781 | solution.py:37
  671.3 3.1 convolution_bitcast_fusion.2
  693.5 3.1 convolution_negate_fusion.1
  711.1 44.5 %fusion.68 = bf16[128,2,8,128]{3,1,0,2:T(2,128)(2,1)S(1)} fusion(f32[8,128,2,128]{3,2,1,0:T(2,128)S(1)} %bitcast.296, f32[8,128,2]{2,1,0:T(8,128)} %copy.214, f32[128,2,8,128]{3,2,1,0:T(8,128)} %copy-done.14), kind=kOutput, calls=%fused_computation.98 | output fusion | flops 1837183 | bytes 2629632 | tf_op jit(solution)/shard_map/mul | solution.py:50
  (299 shorter events, 231.8 us)
Async XLA Ops:
  7.2 226.0 %all-reduce.14.cloned.1.call-start = ((), (), s32[]{:S(2)}) async-start(), calls=%async_computation | async-start | bytes 2097152 | tf_op jit(solution)/shard_map/psum | solution.py:23
  8.5 3.7 copy-start.14
  99.0 144.5 %copy-start.12 = (f32[8,128,256]{2,1,0:T(8,128)}, f32[8,128,256]{2,1,0:T(8,128)S(1)}, u32[]{:S(2)}) copy-start(f32[8,128,256]{2,1,0:T(8,128)S(1)} %fusion.73) | copy-start | bytes 3145732
  186.7 8.4 %copy-start.20 = (f32[8,128,128,1]{2,1,0,3:T(8,128)}, f32[8,128,128,1]{2,1,0,3:T(8,128)S(1)}, u32[]{:S(2)}) copy-start(f32[8,128,128,1]{2,1,0,3:T(8,128)S(1)} %fusion.55) | copy-start | bytes 1572868
  187.8 45.6 %copy-start.5 = (f32[1,8,128,128]{3,2,1,0:T(8,128)}, f32[1,8,128,128]{3,2,1,0:T(8,128)S(1)}, u32[]{:S(2)}) copy-start(f32[1,8,128,128]{3,2,1,0:T(8,128)S(1)} %stack_broadcast_in_dim.7) | copy-start | bytes 1572868
  193.2 3.3 copy-start.23
  195.1 5.2 collective-permute-start
  201.6 31.7 %copy-start.22 = (f32[1,8,128,128]{3,2,1,0:T(8,128)}, f32[1,8,128,128]{3,2,1,0:T(8,128)S(1)}, u32[]{:S(2)}) copy-start(f32[1,8,128,128]{3,2,1,0:T(8,128)S(1)} %get-tuple-element.266) | copy-start | bytes 1572868
  205.0 142.9 %all-gather.3.cloned.1.call-start = ((), (), s32[]{:S(2)}) async-start(), calls=%async_computation.1 | async-start | bytes 17825792 | tf_op jit(solution)/shard_map/all_gather | solution.py:28
  233.2 265.7 %all-reduce.16.cloned.1.call-start = ((), (), s32[]{:S(2)}) async-start(), calls=%async_computation.2 | async-start | bytes 2097152 | tf_op jit(solution)/shard_map/psum | solution.py:23
  240.0 4.9 copy-start.32
  241.3 3.6 copy-start.4
  242.4 209.9 %copy-start.25 = (f32[8,64,128]{2,1,0:T(8,128)}, f32[8,64,128]{2,1,0:T(8,128)S(1)}, u32[]{:S(2)}) copy-start(f32[8,64,128]{2,1,0:T(8,128)S(1)} %convolution_multiply_fusion.5) | copy-start | bytes 786436
  437.7 21.0 %copy-start.31 = (f32[8,64,128]{2,1,0:T(8,128)S(1)}, f32[8,64,128]{2,1,0:T(8,128)}, u32[]{:S(2)}) copy-start(f32[8,64,128]{2,1,0:T(8,128)} %convolution_subtract_fusion.7) | copy-start | bytes 786436
  437.7 22.0 %copy-start.6 = (f32[1,8,128,128]{3,2,1,0:T(8,128)S(1)}, f32[1,8,128,128]{3,2,1,0:T(8,128)}, u32[]{:S(2)}) copy-start(f32[1,8,128,128]{3,2,1,0:T(8,128)} %copy-done.5) | copy-start | bytes 1572868
  437.7 22.0 %copy-start.21 = (f32[8,128,128,1]{2,1,0,3:T(8,128)S(1)}, f32[8,128,128,1]{2,1,0,3:T(8,128)}, u32[]{:S(2)}) copy-start(f32[8,128,128,1]{2,1,0,3:T(8,128)} %copy-done.20) | copy-start | bytes 1572868
  437.7 23.2 %copy-start.30 = (f32[8,64,128]{2,1,0:T(8,128)S(1)}, f32[8,64,128]{2,1,0:T(8,128)}, u32[]{:S(2)}) copy-start(f32[8,64,128]{2,1,0:T(8,128)} %convolution_subtract_fusion.6) | copy-start | bytes 786436
  437.7 24.2 %copy-start.19 = (f32[8,128,128,1]{2,1,0,3:T(8,128)S(1)}, f32[8,128,128,1]{2,1,0,3:T(8,128)}, u32[]{:S(2)}) copy-start(f32[8,128,128,1]{2,1,0,3:T(8,128)} %fusion.50) | copy-start | bytes 1572868
  442.3 64.9 %copy-start = (f32[8,128,128]{2,1,0:T(8,128)}, f32[8,128,128]{2,1,0:T(8,128)S(1)}, u32[]{:S(2)}) copy-start(f32[8,128,128]{2,1,0:T(8,128)S(1)} %fusion.88) | copy-start | bytes 1572868
  444.9 60.1 %copy-start.2 = (f32[8,128,128]{2,1,0:T(8,128)}, f32[8,128,128]{2,1,0:T(8,128)S(1)}, u32[]{:S(2)}) copy-start(f32[8,128,128]{2,1,0:T(8,128)S(1)} %convolution_subtract_fusion.3) | copy-start | bytes 1572868
  445.9 7.1 copy-start.11
  448.5 3.8 copy-start.7
  465.1 4.9 collective-permute-start.1
  473.9 141.2 %all-gather.5.cloned.1.call-start = ((), (), s32[]{:S(2)}) async-start(), calls=%async_computation.3 | async-start | bytes 17825792 | tf_op jit(solution)/shard_map/all_gather | solution.py:28
  671.2 22.3 %copy-start.3 = (f32[8,128,128]{2,1,0:T(8,128)S(1)}, f32[8,128,128]{2,1,0:T(8,128)}, u32[]{:S(2)}) copy-start(f32[8,128,128]{2,1,0:T(8,128)} %copy-done.2) | copy-start | bytes 1572868
  671.2 29.2 %copy-start.1 = (f32[8,128,128]{2,1,0:T(8,128)S(1)}, f32[8,128,128]{2,1,0:T(8,128)}, u32[]{:S(2)}) copy-start(f32[8,128,128]{2,1,0:T(8,128)} %copy-done) | copy-start | bytes 1572868
  674.3 13.2 %copy-start.16 = (f32[2,8,128,128]{3,2,1,0:T(8,128)}, f32[2,8,128,128]{3,2,1,0:T(8,128)S(1)}, u32[]{:S(2)}) copy-start(f32[2,8,128,128]{3,2,1,0:T(8,128)S(1)} %convolution_bitcast_fusion.2) | copy-start | bytes 3145732
  674.4 29.1 %copy-start.8 = (f32[8,128,128]{2,1,0:T(8,128)S(1)}, f32[8,128,128]{2,1,0:T(8,128)}, u32[]{:S(2)}) copy-start(f32[8,128,128]{2,1,0:T(8,128)} %copy-done.7) | copy-start | bytes 1572868
  674.4 29.1 %copy-start.10 = (f32[1,8,128,128]{3,2,1,0:T(8,128)S(1)}, f32[1,8,128,128]{3,2,1,0:T(8,128)}, u32[]{:S(2)}) copy-start(f32[1,8,128,128]{3,2,1,0:T(8,128)} %copy-done.9) | copy-start | bytes 1572868
  674.4 33.0 %copy-start.33 = (f32[128,128]{1,0:T(8,128)S(1)}, f32[128,128]{1,0:T(8,128)}, u32[]{:S(2)}) copy-start(f32[128,128]{1,0:T(8,128)} %get-tuple-element.288) | copy-start | bytes 196612
  678.9 6.2 copy-start.15
  685.1 5.0 copy-start.24
  (9 other events, 11.1 us)
Sparse Core Ops, SparseCore 0:
  205.1 28.0 all-reduce.13
  235.5 112.3 all-gather.2
  474.0 24.8 all-reduce.15
  500.9 114.1 all-gather.4
where the time goes:
time: 773 us; the launch traced here: 764 us
  other arithmetic  223 us (29%)
  matrix products  188 us (24%)
  waiting for transfers between devices  177 us (23%)
  local copies, waits for them, and re-layouts  85.9 us (11%)
  blocking collectives  68.1 us (9%)
  between operations  15 us (2%)
    dot_general x83, matrix products, product(): jnp.einsum(spec, left, right, precision=EXACT, preferred_element_type=jnp...  180 us
    another operation x3, other arithmetic, stretch_factors(): solved = jax.scipy.linalg.solve_triangular(lower_mat, rhs, lower=True)  159 us
    all_gather x2, waiting for transfers between devices, prefix(): everything = lax.all_gather(shard, axis)  118 us
    psum x1, blocking collectives, on_device(): total = lax.psum(gain_sum, ('dp', 'outer', 'inner'))  68.1 us
    psum x2, waiting for transfers between devices, spread(): return lax.psum(kept, axis)  53.1 us
    mul x2, other arithmetic, unit_back(): unit * jnp.sum(unit * grad, axis=-1, keepdims=True)  50.9 us
    slice x34, local copies, waits for them, and re-layouts, compose(): return through + jnp.stack([jnp.zeros_like(later[1]), later[1]])  34.6 us
    while x64, local copies, waits for them, and re-layouts  27 us
  transfers between devices with their start and end apart: 6, of which 6 were waited for; matrix products, arithmetic and copies ran while one was open for 6% of the time, Pallas kernels for 0%

commit v1 on v0

--- a/solution.py
+++ b/solution.py
@@ -240,7 +240,8 @@
         .reshape(1, length_here, 2, heads * head_dim)
         .astype(jnp.bfloat16)
     )
-    total = lax.psum(gain_sum, ("dp", "outer", "inner"))
+    one_axis = lax.psum(gain_sum, "dp")
+    total = lax.psum(one_axis, ("outer", "inner"))
     tokens_all = length_here * lax.axis_size("dp") * lax.axis_size("outer") * lax.axis_size("inner")
     gain_grad = total.reshape(heads * head_dim) * (1.0 / math.sqrt(tokens_all))
     return (grad_q, grad_k, grad_val, gain_grad)

time: 773 us -> 772 us (level)
    psum x1 -> x2, blocking collectives: 68.1 us -> 74.1 us  [the longest x1 64.9 us: on_device(): total = lax.psum(one_axis, ('outer', 'inner'))]
where the time goes in v1:
time: 772 us; the launch traced here: 763 us
  other arithmetic  223 us (29%)
  matrix products  188 us (24%)
  waiting for transfers between devices  170 us (22%)
  local copies, waits for them, and re-layouts  85.9 us (11%)
  blocking collectives  74.1 us (10%)
  between operations  15 us (2%)
    dot_general x83, matrix products, product(): jnp.einsum(spec, left, right, precision=EXACT, preferred_element_type=jnp...  180 us
    another operation x3, other arithmetic, stretch_factors(): solved = jax.scipy.linalg.solve_triangular(lower_mat, rhs, lower=True)  159 us
    all_gather x2, waiting for transfers between devices, prefix(): everything = lax.all_gather(shard, axis)  111 us
    psum x1, blocking collectives, on_device(): total = lax.psum(one_axis, ('outer', 'inner'))  64.9 us
    psum x2, waiting for transfers between devices, spread(): return lax.psum(kept, axis)  53.1 us
    mul x2, other arithmetic, unit_back(): unit * jnp.sum(unit * grad, axis=-1, keepdims=True)  50.8 us
    slice x34, local copies, waits for them, and re-layouts, compose(): return through + jnp.stack([jnp.zeros_like(later[1]), later[1]])  34.6 us
    while x64, local copies, waits for them, and re-layouts  27 us
  transfers between devices with their start and end apart: 6, of which 6 were waited for; matrix products, arithmetic and copies ran while one was open for 6% of the time, Pallas kernels for 0%

profile of v1, /device:TPU:1, one launch (start us, length us, event | category | flops | bytes accessed | tf_op | source)
XLA Modules:
  0.0 762.8 jit_solution(14330309725084646063)
XLA Ops:
  13.9 79.8 %custom-call.9 = f32[8,1,128,128]{2,3,1,0:T(8,128)} custom-call(f32[8,1,128,128]{3,2,1,0:T(8,128)S(1)} %fusion.54), custom_call_target="InvertDiagBlocksLowerTriangular" | custom-call | tf_op jit(solution)/shard_map/jit(_solve_triangular)/vmap()/triangular_solve | solution.py:65
  103.9 79.4 %custom-call.8 = f32[8,1,128,128]{2,3,1,0:T(8,128)} custom-call(f32[8,1,128,128]{3,2,1,0:T(8,128)S(1)} %fusion.59), custom_call_target="InvertDiagBlocksLowerTriangular" | custom-call | tf_op jit(solution)/shard_map/jit(_solve_triangular)/vmap()/triangular_solve | solution.py:65
  196.4 3.9 collective-permute-done
  201.6 3.4 fusion.47
  205.1 28.1 %all-reduce.14.cloned.1.call-done = f32[1,2,8,128,128]{4,3,2,1,0:T(8,128)} async-done(((f32[1,2,8,128,128]{4,3,2,1,0:T(8,128)}), f32[1,2,8,128,128]{4,3,2,1,0:T(8,128)}) %all-reduce.14.cloned.1.call-update) | async-done | bytes 1048592 | tf_op jit(solution)/shard_map/psum | solution.py:23
  247.2 100.7 %all-gather.3.cloned.1.call-done = f32[16,2,8,128,128]{4,3,2,1,0:T(8,128)} async-done(((f32[1,2,8,128,128]{4,3,2,1,0:T(8,128)}), f32[16,2,8,128,128]{4,3,2,1,0:T(8,128)}) %all-gather.3.cloned.1.call-update) | async-done | bytes 16777232 | tf_op jit(solution)/shard_map/all_gather | solution.py:28
  347.9 89.9 %while.28 = (s32[]{:T(128)}, f32[2,8,128,128]{2,3,1,0:T(8,128)}, s32[]{:T(128)}, f32[16,2,8,128,128]{4,3,2,1,0:T(8,128)}, s32[]{:T(128)}, /*index=5*/s32[]{:T(128)}, s32[]{}) while((s32[]{:T(128)}, f32[2,8,128,128]{2,3,1,0:T(8,128)}, s32[]{:T(128)}, f32[16,2,8,128,128]{4,3,2,1,0:T(8,128)}, s32[]{:T(128)}, /*index=5*/s32[]{:T(128)}, s32[]{}) %tuple.94), condition=%wide.region_4.6_spmd, body=%wide.region_3.5_spmd.sunk | while | flops 403177472 | bytes 8389227 | solution.py:37
  350.4 3.1 fusion.235
  356.0 3.1 fusion.235
  361.6 3.1 fusion.235
  367.2 3.1 fusion.235
  372.8 3.1 fusion.235
  378.4 3.1 fusion.235
  384.0 3.1 fusion.235
  389.6 3.1 fusion.235
  395.2 3.1 fusion.235
  400.8 3.1 fusion.235
  406.4 3.1 fusion.235
  412.0 3.1 fusion.235
  417.6 3.1 fusion.235
  423.2 3.1 fusion.235
  428.8 3.1 fusion.235
  434.4 3.1 fusion.235
  437.9 3.5 convolution_bitcast_fusion.5
  474.1 25.0 %all-reduce.16.cloned.1.call-done = f32[1,2,8,128,128]{4,3,2,1,0:T(8,128)} async-done(((f32[1,2,8,128,128]{4,3,2,1,0:T(8,128)}), f32[1,2,8,128,128]{4,3,2,1,0:T(8,128)}) %all-reduce.16.cloned.1.call-update) | async-done | bytes 1048592 | tf_op jit(solution)/shard_map/psum | solution.py:23
  509.6 6.4 fusion.65
  517.7 9.3 %psum.30 = f32[8,128]{1,0:T(8,128)S(1)} all-reduce(f32[8,128]{1,0:T(8,128)S(1)} %add.277), channel_id=1, replica_groups=mesh['dp'=4,'outer'=16,'inner'=2] {'dp'}, use_global_device_ids=true, to_apply=%region_16.19 | all-reduce | flops 1024 | bytes 8192 | tf_op jit(solution)/shard_map/psum | solution.py:243
  527.0 64.9 %psum.31 = f32[8,128]{1,0:T(8,128)S(1)} all-reduce(f32[8,128]{1,0:T(8,128)S(1)} %psum.30), channel_id=1, replica_groups=mesh['dp'=4,'outer'=16,'inner'=2] {'outer','inner'}, use_global_device_ids=true, to_apply=%region_17.20 | all-reduce | flops 1024 | bytes 8192 | tf_op jit(solution)/shard_map/psum | solution.py:244
  603.8 10.2 %all-gather.5.cloned.1.call-done = f32[16,2,8,128,128]{4,3,2,1,0:T(8,128)} async-done(((f32[1,2,8,128,128]{4,3,2,1,0:T(8,128)}), f32[16,2,8,128,128]{4,3,2,1,0:T(8,128)}) %all-gather.5.cloned.1.call-update) | async-done | bytes 16777232 | tf_op jit(solution)/shard_map/all_gather | solution.py:28
  614.0 56.1 %while.29 = (s32[]{:T(128)}, f32[2,8,128,128]{2,3,1,0:T(8,128)S(1)}, s32[]{:T(128)}, f32[16,2,8,128,128]{4,3,2,1,0:T(8,128)}, s32[]{:T(128)}, /*index=5*/s32[]{:T(128)}, s32[]{:T(128)}, s32[]{:T(128)}, s32[]{}) while((s32[]{:T(128)}, f32[2,8,128,128]{2,3,1,0:T(8,128)S(1)}, s32[]{:T(128)}, f32[16,2,8,128,128]{4,3,2,1,0:T(8,128)}, ...), condition=%wide.region_12.14_spmd, body=%wide.region_11.13_spmd.sunk | while | flops 403177472 | bytes 8388781 | solution.py:37
  670.2 3.1 convolution_bitcast_fusion.2
  710.1 44.4 %fusion.68 = bf16[128,2,8,128]{3,1,0,2:T(2,128)(2,1)S(1)} fusion(f32[8,128,2,128]{3,2,1,0:T(2,128)S(1)} %bitcast.296, f32[8,128,2]{2,1,0:T(8,128)} %copy.214, f32[128,2,8,128]{3,2,1,0:T(8,128)} %copy-done.14), kind=kOutput, calls=%fused_computation.98 | output fusion | flops 1837183 | bytes 2629632 | tf_op jit(solution)/shard_map/mul | solution.py:50
  (300 shorter events, 234.9 us)
Async XLA Ops:
  7.2 226.0 %all-reduce.14.cloned.1.call-start = ((), (), s32[]{:S(2)}) async-start(), calls=%async_computation | async-start | bytes 2097152 | tf_op jit(solution)/shard_map/psum | solution.py:23
  8.5 3.7 copy-start.14
  99.0 144.6 %copy-start.12 = (f32[8,128,256]{2,1,0:T(8,128)}, f32[8,128,256]{2,1,0:T(8,128)S(1)}, u32[]{:S(2)}) copy-start(f32[8,128,256]{2,1,0:T(8,128)S(1)} %fusion.73) | copy-start | bytes 3145732
  186.7 8.4 %copy-start.20 = (f32[8,128,128,1]{2,1,0,3:T(8,128)}, f32[8,128,128,1]{2,1,0,3:T(8,128)S(1)}, u32[]{:S(2)}) copy-start(f32[8,128,128,1]{2,1,0,3:T(8,128)S(1)} %fusion.55) | copy-start | bytes 1572868
  187.8 45.6 %copy-start.5 = (f32[1,8,128,128]{3,2,1,0:T(8,128)}, f32[1,8,128,128]{3,2,1,0:T(8,128)S(1)}, u32[]{:S(2)}) copy-start(f32[1,8,128,128]{3,2,1,0:T(8,128)S(1)} %stack_broadcast_in_dim.7) | copy-start | bytes 1572868
  193.2 3.3 copy-start.23
  195.1 5.2 collective-permute-start
  201.6 31.8 %copy-start.22 = (f32[1,8,128,128]{3,2,1,0:T(8,128)}, f32[1,8,128,128]{3,2,1,0:T(8,128)S(1)}, u32[]{:S(2)}) copy-start(f32[1,8,128,128]{3,2,1,0:T(8,128)S(1)} %get-tuple-element.266) | copy-start | bytes 1572868
  205.0 142.9 %all-gather.3.cloned.1.call-start = ((), (), s32[]{:S(2)}) async-start(), calls=%async_computation.1 | async-start | bytes 17825792 | tf_op jit(solution)/shard_map/all_gather | solution.py:28
  233.2 265.9 %all-reduce.16.cloned.1.call-start = ((), (), s32[]{:S(2)}) async-start(), calls=%async_computation.2 | async-start | bytes 2097152 | tf_op jit(solution)/shard_map/psum | solution.py:23
  240.0 4.9 copy-start.32
  241.3 3.6 copy-start.4
  242.4 210.1 %copy-start.25 = (f32[8,64,128]{2,1,0:T(8,128)}, f32[8,64,128]{2,1,0:T(8,128)S(1)}, u32[]{:S(2)}) copy-start(f32[8,64,128]{2,1,0:T(8,128)S(1)} %convolution_multiply_fusion.5) | copy-start | bytes 786436
  437.8 21.0 %copy-start.31 = (f32[8,64,128]{2,1,0:T(8,128)S(1)}, f32[8,64,128]{2,1,0:T(8,128)}, u32[]{:S(2)}) copy-start(f32[8,64,128]{2,1,0:T(8,128)} %convolution_subtract_fusion.7) | copy-start | bytes 786436
  437.9 22.0 %copy-start.6 = (f32[1,8,128,128]{3,2,1,0:T(8,128)S(1)}, f32[1,8,128,128]{3,2,1,0:T(8,128)}, u32[]{:S(2)}) copy-start(f32[1,8,128,128]{3,2,1,0:T(8,128)} %copy-done.5) | copy-start | bytes 1572868
  437.9 22.0 %copy-start.21 = (f32[8,128,128,1]{2,1,0,3:T(8,128)S(1)}, f32[8,128,128,1]{2,1,0,3:T(8,128)}, u32[]{:S(2)}) copy-start(f32[8,128,128,1]{2,1,0,3:T(8,128)} %copy-done.20) | copy-start | bytes 1572868
  437.9 23.2 %copy-start.30 = (f32[8,64,128]{2,1,0:T(8,128)S(1)}, f32[8,64,128]{2,1,0:T(8,128)}, u32[]{:S(2)}) copy-start(f32[8,64,128]{2,1,0:T(8,128)} %convolution_subtract_fusion.6) | copy-start | bytes 786436
  437.9 24.2 %copy-start.19 = (f32[8,128,128,1]{2,1,0,3:T(8,128)S(1)}, f32[8,128,128,1]{2,1,0,3:T(8,128)}, u32[]{:S(2)}) copy-start(f32[8,128,128,1]{2,1,0,3:T(8,128)} %fusion.50) | copy-start | bytes 1572868
  442.5 64.9 %copy-start = (f32[8,128,128]{2,1,0:T(8,128)}, f32[8,128,128]{2,1,0:T(8,128)S(1)}, u32[]{:S(2)}) copy-start(f32[8,128,128]{2,1,0:T(8,128)S(1)} %fusion.88) | copy-start | bytes 1572868
  445.1 60.1 %copy-start.2 = (f32[8,128,128]{2,1,0:T(8,128)}, f32[8,128,128]{2,1,0:T(8,128)S(1)}, u32[]{:S(2)}) copy-start(f32[8,128,128]{2,1,0:T(8,128)S(1)} %convolution_subtract_fusion.3) | copy-start | bytes 1572868
  446.1 7.1 copy-start.11
  448.7 3.8 copy-start.7
  465.3 4.9 collective-permute-start.1
  474.0 140.0 %all-gather.5.cloned.1.call-start = ((), (), s32[]{:S(2)}) async-start(), calls=%async_computation.3 | async-start | bytes 17825792 | tf_op jit(solution)/shard_map/all_gather | solution.py:28
  670.2 22.3 %copy-start.3 = (f32[8,128,128]{2,1,0:T(8,128)S(1)}, f32[8,128,128]{2,1,0:T(8,128)}, u32[]{:S(2)}) copy-start(f32[8,128,128]{2,1,0:T(8,128)} %copy-done.2) | copy-start | bytes 1572868
  670.2 29.2 %copy-start.1 = (f32[8,128,128]{2,1,0:T(8,128)S(1)}, f32[8,128,128]{2,1,0:T(8,128)}, u32[]{:S(2)}) copy-start(f32[8,128,128]{2,1,0:T(8,128)} %copy-done) | copy-start | bytes 1572868
  673.3 13.2 %copy-start.16 = (f32[2,8,128,128]{3,2,1,0:T(8,128)}, f32[2,8,128,128]{3,2,1,0:T(8,128)S(1)}, u32[]{:S(2)}) copy-start(f32[2,8,128,128]{3,2,1,0:T(8,128)S(1)} %convolution_bitcast_fusion.2) | copy-start | bytes 3145732
  673.3 29.0 %copy-start.8 = (f32[8,128,128]{2,1,0:T(8,128)S(1)}, f32[8,128,128]{2,1,0:T(8,128)}, u32[]{:S(2)}) copy-start(f32[8,128,128]{2,1,0:T(8,128)} %copy-done.7) | copy-start | bytes 1572868
  673.3 29.0 %copy-start.10 = (f32[1,8,128,128]{3,2,1,0:T(8,128)S(1)}, f32[1,8,128,128]{3,2,1,0:T(8,128)}, u32[]{:S(2)}) copy-start(f32[1,8,128,128]{3,2,1,0:T(8,128)} %copy-done.9) | copy-start | bytes 1572868
  673.3 33.0 %copy-start.33 = (f32[128,128]{1,0:T(8,128)S(1)}, f32[128,128]{1,0:T(8,128)}, u32[]{:S(2)}) copy-start(f32[128,128]{1,0:T(8,128)} %get-tuple-element.288) | copy-start | bytes 196612
  677.9 6.2 copy-start.15
  684.1 5.0 copy-start.24
  (9 other events, 11.1 us)
Sparse Core Ops, SparseCore 0:
  205.1 28.0 all-reduce.13
  235.5 112.3 all-gather.2
  474.2 24.8 all-reduce.15
  501.1 112.9 all-gather.4
